TPU v7x, 32 devices: a whole 2x2x4 slice. The times are simulated.
32 devices in a mesh: gx: 4 (over y, x), gy: 8 (over z, core).
Axes of the slice: x: 2, y: 2, z: 4, core: 2. Of those that a mesh axis runs over, the one named last changes fastest.
Arguments:
- tiles: bfloat16 [1024, 3, 4096], P(('gx', 'gy'))
- smoother: bfloat16 [1024, 4096], P(('gx', 'gy'))
- rhs: bfloat16 [1024, 2048], P(('gx', 'gy')), may hold values from -6 to 6
- cols: int32 [1024, 3], P(('gx', 'gy')), may hold values from 0 to 1023, as said below
- agg: int32 [1024, 1], P(('gx', 'gy')), may hold values from 0 to 7; in each aligned block of 32 rows (0 to 31, 32 to 63, ...) at most 8 rows name the same one
- coarse_slot: int32 [1024, 3], P(('gx', 'gy')), may hold values from 0 to 3
Outputs:
- iterate: float32 [1024, 2048], P(('gx', 'gy'))
- coarse_residual: float32 [32, 2048], P(('gx', 'gy'))
- coarse_tiles: float32 [32, 4, 4096], P(('gx', 'gy'))
Inputs may be any that keep to these rules, and one draw needn't show every extreme that they name: cols[i, 0] = i; every other slot holds a block row at most 16 away from i, and slot 2 one exactly 16 away. `agg`: in the block rows of one device at most 8 name the same aggregate.
All inputs are finite; a program needn't handle non-finite values.
Results may differ from a plain program's by a relative error of at most 0.00045.
Values may be sent and summed in bfloat16 or wider, within the bound.
A program may use at most 64 MiB of HBM per device.

v0:
```python
import jax
import jax.numpy as jnp
from jax import lax
from jax.sharding import PartitionSpec as P

TILE = 64
NRHS = 32
KC = 4
SWEEPS = 3


def extended(block, sides, width):
    for axis, dim in sides:
        count = lax.axis_size(axis)
        forward = [(i, i + 1) for i in range(count - 1)]
        backward = [(target, source) for source, target in forward]
        low = lax.ppermute(
            lax.slice_in_dim(block, block.shape[dim] - width, None, axis=dim), axis, forward
        )
        high = lax.ppermute(lax.slice_in_dim(block, 0, width, axis=dim), axis, backward)
        block = jnp.concatenate([low, block, high], axis=dim)
    return block


def body(tiles, smoother, rhs, cols, agg, coarse_slot):
    row_count = tiles.shape[0]
    slot_count = tiles.shape[1]
    group_size = lax.axis_size("gy")
    halo_rows = row_count // 2
    tile_wide = tiles.reshape(row_count, slot_count, TILE, TILE).astype(jnp.float32)
    smooth_wide = smoother.reshape(row_count, TILE, TILE).astype(jnp.float32)
    local_cols = cols - (lax.axis_index(("gx", "gy")) * row_count - halo_rows)

    def apply_operator(field):
        padded = extended(field, ((("gx", "gy"), 0),), halo_rows)
        picked = padded.reshape(-1, TILE, NRHS)[local_cols]
        return jnp.einsum("ikrc,ikcj->irj", tile_wide, picked, precision=lax.Precision.HIGHEST)

    def apply_smoother(residual):
        return jnp.einsum("irc,icj->irj", smooth_wide, residual, precision=lax.Precision.HIGHEST)

    aggregate = agg[:, 0]
    keys = (aggregate[:, None] * KC + coarse_slot).reshape(-1)
    partial_sums = jax.ops.segment_sum(
        tiles.reshape(-1, TILE * TILE).astype(jnp.float32), keys, num_segments=group_size * KC
    )
    arrived = lax.all_to_all(
        partial_sums.reshape(group_size, KC, TILE * TILE),
        "gy",
        split_axis=0,
        concat_axis=0,
        tiled=True,
    )
    coarse_tiles = jnp.sum(arrived, axis=0, keepdims=True)
    source = rhs.astype(jnp.float32).reshape(row_count, TILE, NRHS)
    iterate = apply_smoother(source)
    for sweep_index in range(SWEEPS - 1):
        residual = source - apply_operator(iterate.reshape(row_count, TILE * NRHS))
        iterate = iterate + apply_smoother(residual)
    residual = source - apply_operator(iterate.reshape(row_count, TILE * NRHS))
    owner_sums = jax.ops.segment_sum(
        residual.reshape(row_count, TILE * NRHS), aggregate, num_segments=group_size
    )
    coarse_residual = lax.psum_scatter(owner_sums, "gy", scatter_dimension=0, tiled=True)
    return (iterate.reshape(row_count, TILE * NRHS), coarse_residual, coarse_tiles)


def solution(mesh):
    return jax.shard_map(
        body,
        mesh=mesh,
        in_specs=(
            P(("gx", "gy"), None, None),
            P(("gx", "gy"), None),
            P(("gx", "gy"), None),
            P(("gx", "gy"), None),
            P(("gx", "gy"), None),
            P(("gx", "gy"), None),
        ),
        out_specs=(P(("gx", "gy"), None), P(("gx", "gy"), None), P(("gx", "gy"), None, None)),
        check_vma=False,
    )
```

profile of v0, /device:TPU:0, one launch (start us, length us, event | category | flops | bytes accessed | tf_op | source)
XLA Modules:
  0.0 159.9 jit_solution(13314954159925996843)
XLA Ops:
  7.2 1.5 reshape.54
  8.6 1.3 reshape.55
  9.9 0.4 fusion.15
  10.5 0.2 copy.78
  10.7 0.2 slice.37
  10.9 3.0 %collective-permute-start = (f32[16,2048]{1,0:T(8,128)S(1)}, f32[16,2048]{1,0:T(8,128)}, u32[]{:S(2)}, u32[]{:S(2)}) collective-permute-start(f32[16,2048]{1,0:T(8,128)S(1)} %slice.37), channel_id=1, source_target_pairs={{0,1},{1,2},{2,3},{3,4},{4,5},{5,6},{6,7},{7,8},{8,9},{9,10},{10,1... | collective-permute-start | bytes 393224 | tf_op jit(solution)/shard_map/ppermute | solution.py:17
  13.9 0.2 copy.79
  14.2 0.2 slice.39
  14.4 1.3 collective-permute-start.1
  15.8 0.2 copy.77
  16.0 1.7 %reshape.57 = bf16[32,3,64,64]{3,2,0,1:T(8,128)(2,1)S(1)} reshape(bf16[32,3,4096]{2,0,1:T(8,128)(2,1)S(1)} %copy-done.6) | data formatting | bytes 1572864 | tf_op jit(solution)/shard_map/reshape | solution.py:30
  17.7 2.0 %copy.97 = f32[32,3,4096]{2,1,0:T(4,128)} copy(bf16[32,3,4096]{2,0,1:T(8,128)(2,1)S(1)} %copy-done.6) | data formatting | bytes 2359296 | tf_op jit(solution)/shard_map/convert_element_type | solution.py:45
  19.9 2.9 %reshape.98 = f32[96,4096]{1,0:T(8,128)} reshape(f32[32,3,4096]{2,1,0:T(4,128)} %copy.97) | data formatting | bytes 3145728 | tf_op jit(solution)/shard_map/convert_element_type | solution.py:45
  22.9 1.1 concatenate.24
  23.9 0.9 copy.80
  24.8 0.2 concatenate.25
  25.0 0.9 copy.81
  25.9 1.3 pad_maximum_fusion
  27.2 1.9 %gather_fusion = f32[96,64,32]{1,2,0:T(8,128)} fusion(f32[64,64,32]{1,2,0:T(8,128)S(1)} %pad_maximum_fusion, s32[1024]{0:T(1024)S(1)} %pad_clamp_fusion), kind=kCustom, calls=%fused_computation | custom fusion | bytes 1573248 | tf_op jit(solution)/shard_map/gather | solution.py:36
  29.1 3.2 %fusion.4 = f32[32,64,32]{1,2,0:T(8,128)S(1)} fusion(f32[32,3,64,32]{2,3,1,0:T(8,128)} %bitcast.49, bf16[32,3,64,64]{3,2,0,1:T(8,128)(2,1)S(1)} %reshape.57, bf16[32,64,32]{1,2,0:T(8,128)(2,1)S(1)} %copy.77), kind=kOutput, calls=%fused_computation.14 | convolution fusion | flops 151126016 | bytes 1966080 | tf_op jit(solution)/shard_map/ikrc,ikcj->irj/dot_general | solution.py:37
  32.3 0.9 fusion.3
  33.3 0.8 copy-done.4
  34.1 0.2 copy.84
  34.3 0.2 slice.41
  34.6 4.6 %collective-permute-start.2 = (f32[16,2048]{1,0:T(8,128)S(1)}, f32[16,2048]{1,0:T(8,128)S(1)}, u32[]{:S(2)}, u32[]{:S(2)}) collective-permute-start(f32[16,2048]{1,0:T(8,128)S(1)} %slice.41), channel_id=1, source_target_pairs={{0,1},{1,2},{2,3},{3,4},{4,5},{5,6},{6,7},{7,8},{8,9},{9,10},{10,1... | collective-permute-start | bytes 393224 | tf_op jit(solution)/shard_map/ppermute | solution.py:17
  39.2 0.2 copy.85
  39.4 0.2 slice.43
  39.6 1.3 collective-permute-start.3
  41.1 3.6 %scatter_custom_fusion.1 = f32[32,4096]{1,0:T(8,128)S(1)} fusion(s32[96]{0:T(128)S(1)} %reshape.96, f32[96,4096]{1,0:T(8,128)} %reshape.98, f32[]{:T(128)} %constant.8.clone.1), kind=kCustom, calls=%fused_computation.21 | custom fusion | flops 393216 | bytes 524800 | tf_op jit(solution)/shard_map/scatter-add | solution.py:44
  44.7 0.9 reshape.60
  45.7 9.1 %all-to-all-start = ((f32[8,4,4096]{2,1,0:T(4,128)}), f32[8,4,4096]{2,1,0:T(4,128)}, u32[]{:S(2)}, u32[]{:S(2)}) async-start(f32[8,4,4096]{2,1,0:T(4,128)} %reshape.60), calls=%async_computation | async-start | bytes 1048576 | tf_op jit(solution)/shard_map/all_to_all | solution.py:47
  54.8 0.2 all-reduce.3.cloned.1.call-start
  55.0 0.2 concatenate.27
  55.2 0.9 copy.86
  56.1 0.2 concatenate.28
  56.2 0.9 copy.87
  57.2 1.3 pad_maximum_fusion.1
  58.4 1.9 %gather_fusion.1 = f32[96,64,32]{1,2,0:T(8,128)} fusion(f32[64,64,32]{1,2,0:T(8,128)S(1)} %pad_maximum_fusion.1, s32[1024]{0:T(1024)S(1)} %pad_clamp_fusion), kind=kCustom, calls=%fused_computation.1 | custom fusion | bytes 1573248 | tf_op jit(solution)/shard_map/gather | solution.py:36
  60.3 3.2 %fusion.2 = f32[32,64,32]{1,2,0:T(8,128)S(1)} fusion(f32[32,3,64,32]{2,3,1,0:T(8,128)} %bitcast.50, bf16[32,3,64,64]{3,2,0,1:T(8,128)(2,1)S(1)} %reshape.57, bf16[32,64,32]{1,2,0:T(8,128)(2,1)S(1)} %copy.77), kind=kOutput, calls=%fused_computation.10 | convolution fusion | flops 151126016 | bytes 1966080 | tf_op jit(solution)/shard_map/ikrc,ikcj->irj/dot_general | solution.py:37
  63.6 0.9 fusion.1
  64.5 0.8 copy-done.2
  65.4 0.2 copy.90
  65.6 0.2 slice.45
  65.8 2.2 %collective-permute-start.4 = (f32[16,2048]{1,0:T(8,128)S(1)}, f32[16,2048]{1,0:T(8,128)S(1)}, u32[]{:S(2)}, u32[]{:S(2)}) collective-permute-start(f32[16,2048]{1,0:T(8,128)S(1)} %slice.45), channel_id=1, source_target_pairs={{0,1},{1,2},{2,3},{3,4},{4,5},{5,6},{6,7},{7,8},{8,9},{9,10},{10,1... | collective-permute-start | bytes 393224 | tf_op jit(solution)/shard_map/ppermute | solution.py:17
  68.0 0.2 copy.91
  68.2 0.2 slice.47
  68.5 1.4 collective-permute-start.5
  69.9 0.2 concatenate.30
  70.1 0.9 copy.92
  71.0 2.0 %collective-permute-done.5 = f32[16,2048]{1,0:T(8,128)S(1)} collective-permute-done((f32[16,2048]{1,0:T(8,128)S(1)}, f32[16,2048]{1,0:T(8,128)S(1)}, u32[]{:S(2)}, u32[]{:S(2)}) %collective-permute-start.5) | collective-permute-done | bytes 131104 | tf_op jit(solution)/shard_map/ppermute | solution.py:20
  73.0 0.2 concatenate.31
  73.1 0.9 copy.93
  74.1 1.1 pad_maximum_fusion.2
  75.2 1.9 %gather_fusion.2 = f32[96,64,32]{1,2,0:T(8,128)} fusion(f32[64,64,32]{1,2,0:T(8,128)S(1)} %pad_maximum_fusion.2, s32[1024]{0:T(1024)S(1)} %pad_clamp_fusion), kind=kCustom, calls=%fused_computation.2 | custom fusion | bytes 1573248 | tf_op jit(solution)/shard_map/gather | solution.py:36
  77.1 4.0 %fusion = f32[32,64,32]{1,2,0:T(8,128)} fusion(f32[32,3,64,32]{2,3,1,0:T(8,128)} %bitcast.48, bf16[32,3,64,64]{3,2,0,1:T(8,128)(2,1)S(1)} %reshape.57, bf16[32,64,32]{1,2,0:T(8,128)(2,1)S(1)} %copy.77), kind=kOutput, calls=%fused_computation.6 | convolution fusion | flops 151126016 | bytes 1966080 | tf_op jit(solution)/shard_map/ikrc,ikcj->irj/dot_general | solution.py:37
  81.0 1.4 copy.95
  82.4 0.5 reshape.90
  82.9 1.6 scatter_custom_fusion
  84.5 0.6 dynamic-slice
  85.1 0.4 copy.89
  85.4 1.2 reshape.58
  86.6 62.7 %all-reduce.3.cloned.1.call-done = f32[8,2048]{1,0:T(8,128)} async-done(((f32[8,2048]{1,0:T(8,128)}), f32[8,2048]{1,0:T(8,128)}) %all-reduce.3.cloned.1.call-update) | async-done | bytes 65552
  149.3 2.0 %constant_dynamic-slice_fusion = f32[1,2048]{1,0:T(1,128)} fusion(f32[8,2048]{1,0:T(8,128)} %all-reduce.3.cloned.1.call-done, u32[]{:T(128)} %bitcast.20), kind=kLoop, calls=%fused_computation.28 | loop fusion | bytes 16388
  151.3 1.8 %reduce_sum.9 = f32[4,4096]{1,0:T(4,128)} reduce(f32[8,4,4096]{2,1,0:T(4,128)} %all-to-all-done, f32[]{:T(128)} %constant.8.clone.1), dimensions={0}, to_apply=%region_3.0 | reduce | flops 114688 | bytes 589828 | tf_op jit(solution)/shard_map/reduce_sum | solution.py:54
  (38 shorter events, 0.6 us)
Async XLA Ops:
  10.4 3.8 %copy-start = (f32[32,64,32]{1,2,0:T(8,128)}, f32[32,64,32]{1,2,0:T(8,128)S(1)}, u32[]{:S(2)}) copy-start(f32[32,64,32]{1,2,0:T(8,128)S(1)} %fusion.15) | copy-start | bytes 786436
  10.4 5.3 %copy-start.7 = (s32[32,3]{0,1:T(4,128)S(1)}, s32[32,3]{0,1:T(4,128)}, u32[]{:S(2)}) copy-start(s32[32,3]{0,1:T(4,128)} %param.9) | copy-start | bytes 1156
  10.4 5.3 %copy-start.9 = (s32[32,1]{0,1:T(1,128)S(1)}, s32[32,1]{0,1:T(1,128)}, u32[]{:S(2)}) copy-start(s32[32,1]{0,1:T(1,128)} %param.10) | copy-start | bytes 388
  10.7 5.3 %copy-start.6 = (bf16[32,3,4096]{2,0,1:T(8,128)(2,1)S(1)}, bf16[32,3,4096]{2,0,1:T(8,128)(2,1)}, u32[]{:S(2)}) copy-start(bf16[32,3,4096]{2,0,1:T(8,128)(2,1)} %param.6) | copy-start | bytes 2359300
  10.9 11.9 %collective-permute-start = (f32[16,2048]{1,0:T(8,128)S(1)}, f32[16,2048]{1,0:T(8,128)}, u32[]{:S(2)}, u32[]{:S(2)}) collective-permute-start(f32[16,2048]{1,0:T(8,128)S(1)} %slice.37), channel_id=1, source_target_pairs={{0,1},{1,2},{2,3},{3,4},{4,5},{5,6},{6,7},{7,8},{8,9},{9,10},{10,1... | collective-permute-start | bytes 393224 | tf_op jit(solution)/shard_map/ppermute | solution.py:17
  14.4 10.4 %collective-permute-start.1 = (f32[16,2048]{1,0:T(8,128)S(1)}, f32[16,2048]{1,0:T(8,128)S(1)}, u32[]{:S(2)}, u32[]{:S(2)}) collective-permute-start(f32[16,2048]{1,0:T(8,128)S(1)} %slice.39), channel_id=1, source_target_pairs={{1,0},{2,1},{3,2},{4,3},{5,4},{6,5},{7,6},{8,7},{9,8},{10,9},{11,1... | collective-permute-start | bytes 393224 | tf_op jit(solution)/shard_map/ppermute | solution.py:20
  29.1 3.2 %copy-start.1 = (f32[32,64,32]{1,2,0:T(8,128)S(1)}, f32[32,64,32]{1,2,0:T(8,128)}, u32[]{:S(2)}) copy-start(f32[32,64,32]{1,2,0:T(8,128)} %copy-done) | copy-start | bytes 786436
  33.3 0.8 copy-start.4
  34.1 6.8 %copy-start.8 = (s32[32,3]{0,1:T(4,128)S(1)}, s32[32,3]{0,1:T(4,128)}, u32[]{:S(2)}) copy-start(s32[32,3]{0,1:T(4,128)} %param.11) | copy-start | bytes 1156
  34.6 20.4 %collective-permute-start.2 = (f32[16,2048]{1,0:T(8,128)S(1)}, f32[16,2048]{1,0:T(8,128)S(1)}, u32[]{:S(2)}, u32[]{:S(2)}) collective-permute-start(f32[16,2048]{1,0:T(8,128)S(1)} %slice.41), channel_id=1, source_target_pairs={{0,1},{1,2},{2,3},{3,4},{4,5},{5,6},{6,7},{7,8},{8,9},{9,10},{10,1... | collective-permute-start | bytes 393224 | tf_op jit(solution)/shard_map/ppermute | solution.py:17
  39.6 16.5 %collective-permute-start.3 = (f32[16,2048]{1,0:T(8,128)S(1)}, f32[16,2048]{1,0:T(8,128)S(1)}, u32[]{:S(2)}, u32[]{:S(2)}) collective-permute-start(f32[16,2048]{1,0:T(8,128)S(1)} %slice.43), channel_id=1, source_target_pairs={{1,0},{2,1},{3,2},{4,3},{5,4},{6,5},{7,6},{8,7},{9,8},{10,9},{11,1... | collective-permute-start | bytes 393224 | tf_op jit(solution)/shard_map/ppermute | solution.py:20
  45.7 105.7 %all-to-all-start = ((f32[8,4,4096]{2,1,0:T(4,128)}), f32[8,4,4096]{2,1,0:T(4,128)}, u32[]{:S(2)}, u32[]{:S(2)}) async-start(f32[8,4,4096]{2,1,0:T(4,128)} %reshape.60), calls=%async_computation | async-start | bytes 1048576 | tf_op jit(solution)/shard_map/all_to_all | solution.py:47
  54.8 94.6 %all-reduce.3.cloned.1.call-start = ((), (), s32[]{:S(2)}) async-start(), calls=%async_computation.1 | async-start | bytes 131072
  60.3 3.2 %copy-start.5 = (f32[32,64,32]{1,2,0:T(8,128)S(1)}, f32[32,64,32]{1,2,0:T(8,128)}, u32[]{:S(2)}) copy-start(f32[32,64,32]{1,2,0:T(8,128)} %copy-done.4) | copy-start | bytes 786436
  64.5 0.8 copy-start.2
  65.8 4.1 %collective-permute-start.4 = (f32[16,2048]{1,0:T(8,128)S(1)}, f32[16,2048]{1,0:T(8,128)S(1)}, u32[]{:S(2)}, u32[]{:S(2)}) collective-permute-start(f32[16,2048]{1,0:T(8,128)S(1)} %slice.45), channel_id=1, source_target_pairs={{0,1},{1,2},{2,3},{3,4},{4,5},{5,6},{6,7},{7,8},{8,9},{9,10},{10,1... | collective-permute-start | bytes 393224 | tf_op jit(solution)/shard_map/ppermute | solution.py:17
  68.5 5.6 %copy-start.3 = (f32[32,64,32]{1,2,0:T(8,128)S(1)}, f32[32,64,32]{1,2,0:T(8,128)}, u32[]{:S(2)}) copy-start(f32[32,64,32]{1,2,0:T(8,128)} %copy-done.2) | copy-start | bytes 786436
  68.5 4.5 %collective-permute-start.5 = (f32[16,2048]{1,0:T(8,128)S(1)}, f32[16,2048]{1,0:T(8,128)S(1)}, u32[]{:S(2)}, u32[]{:S(2)}) collective-permute-start(f32[16,2048]{1,0:T(8,128)S(1)} %slice.47), channel_id=1, source_target_pairs={{1,0},{2,1},{3,2},{4,3},{5,4},{6,5},{7,6},{8,7},{9,8},{10,9},{11,1... | collective-permute-start | bytes 393224 | tf_op jit(solution)/shard_map/ppermute | solution.py:20
  81.0 3.5 %copy-start.10 = (u32[32]{0:T(128)S(1)}, u32[32]{0:T(128)}, u32[]{:S(2)}) copy-start(u32[32]{0:T(128)} %constant.27) | copy-start | bytes 388
Sparse Core Ops, SparseCore 0:
  84.6 64.6 all-reduce.2
where the time goes:
time: 161 us; the launch traced here: 160 us
  waiting for transfers between devices  64.7 us (40%)
  local copies, waits for them, and re-layouts  34.3 us (21%)
  starting transfers between devices  23.1 us (14%)
  between operations  14.4 us (9%)
  matrix products  12.8 us (8%)
  other arithmetic  10.6 us (7%)
    unnamed x2, waiting for transfers between devices  62.7 us
    dot_general x3, matrix products, apply_operator(): jnp.einsum('ikrc,ikcj->irj', tile_wide, picked, precision=lax.Precision.H...  10.4 us
    ppermute x3, starting transfers between devices, extended(): lax.ppermute(lax.slice_in_dim(block, block.shape[dim] - width, None, axis...  9.79 us
    all_to_all x1, starting transfers between devices, body(): lax.all_to_all(partial_sums.reshape(group_size, KC, TILE * TILE), 'gy', s...  9.11 us
    concatenate x12, local copies, waits for them, and re-layouts, extended(): block = jnp.concatenate([low, block, high], axis=dim)  7.31 us
    gather x3, local copies, waits for them, and re-layouts, apply_operator(): picked = padded.reshape(-1, TILE, NRHS)[local_cols]  5.66 us
    convert_element_type x2, local copies, waits for them, and re-layouts, body(): tiles.reshape(-1, TILE * TILE).astype(jnp.float32)  4.92 us
    unnamed x24, local copies, waits for them, and re-layouts  4.17 us
  transfers between devices with their start and end apart: 8, of which 2 were waited for; matrix products, arithmetic and copies ran while one was open for 26% of the time, Pallas kernels for 0%

commit v1 on v0

v1 whole, which is shorter than its diff:
```python
import functools

import jax
import jax.numpy as jnp
from jax import lax
from jax.experimental import pallas as pl
from jax.experimental.pallas import tpu as pltpu
from jax.sharding import PartitionSpec as P

TILE = 64
NRHS = 32
KC = 4
SWEEPS = 3
LANES = 128
PACK = LANES // NRHS
MESH = pl.DeviceIdType.MESH


def split(value):
    high = value.astype(jnp.bfloat16)
    low = (value - high.astype(jnp.float32)).astype(jnp.bfloat16)
    return high, low


def dot(a, b):
    return jnp.dot(a, b, preferred_element_type=jnp.float32)


def kernel(
    n_gx, n_gy, rows,
    cols_ref, agg_ref, keys_ref, flat_ref, tt_ref, ss_ref, b_ref,
    x_out, cr_out, ct_out,
    xs, xh, halo, xb, rb, acc, rq, part, pair, tin, racc, rin,
    halo_send, halo_recv, pair_send, pair_recv, tile_send, tile_recv, res_send, res_recv,
):
    gx, gy = lax.axis_index("gx"), lax.axis_index("gy")
    me = gx * n_gy + gy
    total = n_gx * n_gy
    half = rows // 2
    groups = rows // PACK
    hgroups = groups // 2
    n_par = n_gy // 2
    parity, mine = lax.rem(gy, 2), lax.div(gy, 2)
    has_left, has_right = me > 0, me < total - 1
    left = (lax.div(me + total - 1, n_gy) % n_gx, lax.rem(me + total - 1, n_gy))
    right = (lax.div(me + 1, n_gy) % n_gx, lax.rem(me + 1, n_gy))
    far_left = jnp.logical_and(gy == 0, gx > 0)
    far_right = jnp.logical_and(gy == n_gy - 1, gx < n_gx - 1)

    barrier = pltpu.get_barrier_semaphore()

    def greet(d, carry):
        pl.semaphore_signal(barrier, inc=1, device_id=(gx, lax.rem(gy + d, n_gy)), device_id_type=MESH)
        return carry

    lax.fori_loop(1, n_gy, greet, 0)

    @pl.when(far_left)
    def _():
        pl.semaphore_signal(barrier, inc=1, device_id=left, device_id_type=MESH)

    @pl.when(far_right)
    def _():
        pl.semaphore_signal(barrier, inc=1, device_id=right, device_id_type=MESH)

    def halo_copy(step, side):
        groups_sent = pl.ds(0, hgroups) if side == 0 else pl.ds(hgroups, hgroups)
        return pltpu.make_async_remote_copy(
            src_ref=xh.at[step, groups_sent],
            dst_ref=halo.at[step, 1 - side],
            send_sem=halo_send.at[step, side],
            recv_sem=halo_recv.at[step, 1 - side],
            device_id=left if side == 0 else right,
            device_id_type=MESH,
        )

    def unpack(packed, first):
        for e in range(PACK):
            xb[first + e] = packed[:, e * NRHS:(e + 1) * NRHS]

    def update(step, side):
        start = side * half
        for g in range(side * hgroups, (side + 1) * hgroups):
            gained = []
            for e in range(PACK):
                i = g * PACK + e
                if step == 0:
                    gained.append(dot(ss_ref[i][:, :TILE], b_ref[i]))
                else:
                    gained.append(dot(ss_ref[i], rb[i]))
            value = jnp.concatenate(gained, axis=1)
            if step > 0:
                value = xs[step - 1, g] + value
            xs[step, g] = value
            high, low = split(value)
            xh[step, g] = jnp.concatenate([high, low], axis=0)

    def send_halo(step, side):
        @pl.when(has_left if side == 0 else has_right)
        def _():
            halo_copy(step, side).start()

    def local_part(step):
        for g in range(groups):
            unpack(xh[step, g], half + g * PACK)
        for i in range(rows):
            acc[i] = b_ref[i].astype(jnp.float32) - dot(tt_ref[i], xb[half + i])

    def receive_halo(step):
        for side in range(2):
            @pl.when(has_right if side == 0 else has_left)
            def _():
                halo_copy(step, side).wait_recv()

        for side in range(2):
            for g in range(hgroups):
                unpack(halo[step, side, g], (0 if side == 0 else half + rows) + g * PACK)

    def residual(i):
        one = cols_ref[i, 1]
        two = cols_ref[i, 2]
        return (
            acc[i]
            - dot(tt_ref[rows + i], xb[one])
            - dot(tt_ref[2 * rows + i], xb[two])
        )

    for side in range(2):
        update(0, side)
        if side == 0:
            waits = n_gy - 1 + far_left.astype(jnp.int32) + far_right.astype(jnp.int32)
            pl.semaphore_wait(barrier, waits)

            @pl.when(jnp.logical_not(has_left))
            def _():
                halo[:, 0] = jnp.zeros_like(halo[:, 0])

            @pl.when(jnp.logical_not(has_right))
            def _():
                halo[:, 1] = jnp.zeros_like(halo[:, 1])
        send_halo(0, side)

    n_keys = n_gy * KC
    slots = lax.broadcasted_iota(jnp.int32, (n_keys, 3 * rows), 0)
    chosen = jnp.where(slots == keys_ref[...], 1.0, 0.0).astype(jnp.bfloat16)
    width = 1024
    for at in range(0, TILE * TILE, width):
        sums = dot(chosen, flat_ref[:, at:at + width])
        for p in range(2):
            for q in range(n_par):
                row = (p * n_par + q) * KC
                part[p, q, :, at:at + width] = sums[row:row + KC]
    pair_copy = pltpu.make_async_remote_copy(
        src_ref=part.at[1 - parity],
        dst_ref=pair,
        send_sem=pair_send,
        recv_sem=pair_recv,
        device_id=(gx, 2 * mine + 1 - parity),
        device_id_type=MESH,
    )
    pair_copy.start()

    def tile_copy(d):
        target = lax.rem(mine + d, n_par)
        return pltpu.make_async_remote_copy(
            src_ref=part.at[parity, target],
            dst_ref=tin.at[d - 1],
            send_sem=tile_send.at[d - 1],
            recv_sem=tile_recv.at[d - 1],
            device_id=(gx, 2 * target + parity),
            device_id_type=MESH,
        )

    def res_copy(d):
        target = lax.rem(gy + d, n_gy)
        return pltpu.make_async_remote_copy(
            src_ref=racc.at[target],
            dst_ref=rin.at[d - 1],
            send_sem=res_send.at[d - 1],
            recv_sem=res_recv.at[d - 1],
            device_id=(gx, target),
            device_id_type=MESH,
        )

    def each(first, last, act):
        def one(d, carry):
            act(d)
            return carry

        lax.fori_loop(first, last, one, 0)

    for step in range(SWEEPS - 1):
        local_part(step)
        receive_halo(step)
        for i in range(rows):
            high, low = split(residual(i))
            rb[i] = jnp.concatenate([high, low], axis=0)
        for side in range(2):
            update(step + 1, side)
            send_halo(step + 1, side)
        if step == 0:
            pair_copy.wait_recv()

            def join(q):
                part[parity, q] = part[parity, q] + pair[q]

            each(0, n_par, join)
            each(1, n_par, lambda d: tile_copy(d).start())

    last = SWEEPS - 1
    for g in range(groups):
        for e in range(PACK):
            x_out[g * PACK + e] = xs[last, g, :, e * NRHS:(e + 1) * NRHS]
    local_part(last)
    receive_halo(last)
    quarter = TILE // PACK
    for i in range(rows):
        value = residual(i)
        rq[i] = jnp.concatenate([value[e * quarter:(e + 1) * quarter] for e in range(PACK)], axis=1)

    def gather(a):
        value = jnp.zeros((quarter, LANES), jnp.float32)
        for i in range(rows):
            value = value + jnp.where(agg_ref[i, 0] == a, 1.0, 0.0) * rq[i]
        racc[a] = value

    each(0, n_gy, gather)
    each(1, n_gy, lambda d: res_copy(d).start())

    ct_out[...] = part[parity, mine]

    def add_tiles(d):
        tile_copy(d).wait_recv()
        ct_out[...] = ct_out[...] + tin[d - 1]

    each(1, n_par, add_tiles)

    racc_mine = racc[gy]

    def add_res(d, value):
        res_copy(d).wait_recv()
        return value + rin[d - 1]

    final = lax.fori_loop(1, n_gy, add_res, racc_mine)
    for e in range(PACK):
        cr_out[e * quarter:(e + 1) * quarter, :] = final[:, e * NRHS:(e + 1) * NRHS]

    for step in range(SWEEPS):
        for side in range(2):
            @pl.when(has_left if side == 0 else has_right)
            def _():
                halo_copy(step, side).wait_send()
    pair_copy.wait_send()
    each(1, n_par, lambda d: tile_copy(d).wait_send())
    each(1, n_gy, lambda d: res_copy(d).wait_send())


def body(n_gx, n_gy, tiles, smoother, rhs, cols, agg, coarse_slot):
    rows = tiles.shape[0]
    n_par = n_gy // 2
    groups = rows // PACK
    flat = tiles.transpose(1, 0, 2).reshape(rows * 3, TILE * TILE)
    square = flat.reshape(rows * 3, TILE, TILE)
    double = jnp.concatenate([square, square], axis=2)
    smooth = smoother.reshape(rows, TILE, TILE)
    smooth = jnp.concatenate([smooth, smooth], axis=2)
    source = rhs.reshape(rows, TILE, NRHS)
    places = cols - (lax.axis_index(("gx", "gy")) * rows - rows // 2)
    order = (agg % 2) * n_par + agg // 2
    keys = (order * KC + coarse_slot).T.reshape(1, rows * 3)
    vmem = pl.BlockSpec(memory_space=pltpu.VMEM)
    smem = pl.BlockSpec(memory_space=pltpu.SMEM)
    quarter = TILE // PACK
    f32, bf16 = jnp.float32, jnp.bfloat16
    dma = pltpu.SemaphoreType.DMA
    iterate, residual, coarse = pl.pallas_call(
        functools.partial(kernel, n_gx, n_gy, rows),
        out_shape=(
            jax.ShapeDtypeStruct((rows, TILE, NRHS), f32),
            jax.ShapeDtypeStruct((TILE, NRHS), f32),
            jax.ShapeDtypeStruct((KC, TILE * TILE), f32),
        ),
        in_specs=[smem, smem, vmem, vmem, vmem, vmem, vmem],
        out_specs=(vmem, vmem, vmem),
        scratch_shapes=[
            pltpu.VMEM((SWEEPS, groups, TILE, LANES), f32),
            pltpu.VMEM((SWEEPS, groups, 2 * TILE, LANES), bf16),
            pltpu.VMEM((SWEEPS, 2, groups // 2, 2 * TILE, LANES), bf16),
            pltpu.VMEM((2 * rows, 2 * TILE, NRHS), bf16),
            pltpu.VMEM((rows, 2 * TILE, NRHS), bf16),
            pltpu.VMEM((rows, TILE, NRHS), f32),
            pltpu.VMEM((rows, quarter, LANES), f32),
            pltpu.VMEM((2, n_par, KC, TILE * TILE), f32),
            pltpu.VMEM((n_par, KC, TILE * TILE), f32),
            pltpu.VMEM((n_par - 1, KC, TILE * TILE), f32),
            pltpu.VMEM((n_gy, quarter, LANES), f32),
            pltpu.VMEM((n_gy - 1, quarter, LANES), f32),
            dma((SWEEPS, 2)), dma((SWEEPS, 2)), dma, dma,
            dma((n_par - 1,)), dma((n_par - 1,)), dma((n_gy - 1,)), dma((n_gy - 1,)),
        ],
        compiler_params=pltpu.CompilerParams(
            collective_id=0, has_side_effects=True, vmem_limit_bytes=50 * 1024 * 1024
        ),
    )(places, agg, keys, flat, double, smooth, source)
    return (
        iterate.reshape(rows, TILE * NRHS),
        residual.reshape(1, TILE * NRHS),
        coarse.reshape(1, KC, TILE * TILE),
    )


def solution(mesh):
    row_spec = P(("gx", "gy"), None)
    tile_spec = P(("gx", "gy"), None, None)
    return jax.shard_map(
        functools.partial(body, mesh.shape["gx"], mesh.shape["gy"]),
        mesh=mesh,
        in_specs=(tile_spec, row_spec, row_spec, row_spec, row_spec, row_spec),
        out_specs=(row_spec, row_spec, tile_spec),
        check_vma=False,
    )
```

time: 161 us -> 41.7 us (0.26)
  waiting for transfers between devices: 64.7 us -> 0 us
  Pallas kernels: 0 us -> 31.5 us
  local copies, waits for them, and re-layouts: 34.3 us -> 6.92 us
  starting transfers between devices: 23.1 us -> 0 us
  between operations: 14.4 us -> 0.73 us
  matrix products: 12.8 us -> 0 us
  other arithmetic: 10.6 us -> 2.35 us
    unnamed x2 -> x0, waiting for transfers between devices: 62.7 us -> none
    pallas_call x0 -> x1, Pallas kernels: none -> 31.5 us  [body(): pl.pallas_call(functools.partial(kernel, n_gx, n_gy, rows), out_shape=(ja...]
    ppermute x6 -> x0, starting transfers between devices: 13.8 us -> none  [the longest x3 9.79 us: extended(): lax.ppermute(lax.slice_in_dim(block, block.shape[dim] - width, None, axis...]
    dot_general x6 -> x0, matrix products: 12.8 us -> none  [the longest x3 10.4 us: apply_operator(): jnp.einsum('ikrc,ikcj->irj', tile_wide, picked, precision=lax.Precision.H...]
    all_to_all x1 -> x0, starting transfers between devices: 9.11 us -> none  [body(): lax.all_to_all(partial_sums.reshape(group_size, KC, TILE * TILE), 'gy', s...]
    concatenate x12 -> x0, local copies, waits for them, and re-layouts: 7.31 us -> none  [extended(): block = jnp.concatenate([low, block, high], axis=dim)]
    gather x3 -> x0, local copies, waits for them, and re-layouts: 5.66 us -> none  [apply_operator(): picked = padded.reshape(-1, TILE, NRHS)[local_cols]]
    scatter-add x2 -> x0, other arithmetic: 5.13 us -> none  [the longest x1 3.57 us: body(): jax.ops.segment_sum(tiles.reshape(-1, TILE * TILE).astype(jnp.float32), k...]
  transfers between devices with their start and end apart: 8 -> 0, of which waited for: 2 -> 0; matrix products, arithmetic and copies ran while one was open for 26% -> 0% of each run, Pallas kernels for 0% -> 0%
where the time goes in v1:
time: 41.7 us; the launch traced here: 41.5 us
  Pallas kernels  31.5 us (76%)
  local copies, waits for them, and re-layouts  6.92 us (17%)
  other arithmetic  2.35 us (6%)
  between operations  0.73 us (2%)
    pallas_call x1, Pallas kernels, body(): pl.pallas_call(functools.partial(kernel, n_gx, n_gy, rows), out_shape=(ja...  31.5 us
    another operation x1, local copies, waits for them, and re-layouts, body(): square = flat.reshape(rows * 3, TILE, TILE)  2.52 us
    concatenate x1, other arithmetic, body(): double = jnp.concatenate([square, square], axis=2)  2.03 us
    unnamed x13, local copies, waits for them, and re-layouts  1.54 us
    reshape x1, local copies, waits for them, and re-layouts, body(): iterate.reshape(rows, TILE * NRHS)  1.2 us

profile of v1, /device:TPU:0, one launch (start us, length us, event | category | flops | bytes accessed | tf_op | source)
XLA Modules:
  0.0 41.5 jit_solution(3025575810711790532)
XLA Ops:
  0.6 0.8 %copy.13 = s32[32,3]{1,0:T(8,128)S(1)} copy(s32[32,3]{0,1:T(4,128)} %param.9) | data formatting | bytes 768 | tf_op args[3]
  1.4 2.5 %reshape_reshape.3 = bf16[96,64,64]{2,1,0:T(8,128)(2,1)S(1)} reshape(bf16[3,32,4096]{2,1,0:T(8,128)(2,1)} %bitcast.8) | data formatting | bytes 1572864 | tf_op jit(solution)/shard_map/reshape;reshape | solution.py:263
  3.9 0.0 copy-start.1
  3.9 2.0 %pad_maximum_fusion.tt_ref = bf16[96,64,128]{2,1,0:T(8,128)(2,1)} fusion(bf16[96,64,64]{2,1,0:T(8,128)(2,1)S(1)} %reshape_reshape.3), kind=kLoop, calls=%fused_computation | loop fusion | flops 3145728 | bytes 2359296 | tf_op jit(solution)/shard_map/concatenate | solution.py:264
  6.0 0.0 copy-done.1
  6.0 0.0 copy-start.2
  6.0 0.0 copy-start.4
  6.0 0.0 copy-start.3
  6.0 0.0 copy-start
  6.0 0.5 %reshape.29 = bf16[32,64,64]{2,1,0:T(8,128)(2,1)S(1)} reshape(bf16[32,4096]{1,0:T(8,128)(2,1)S(1)} %copy-done.1) | data formatting | bytes 524288 | tf_op jit(solution)/shard_map/reshape | solution.py:265
  6.5 0.3 pad_maximum_fusion.1.ss_ref
  6.8 0.0 copy-done.2
  6.9 0.4 reshape.30.b_ref
  7.3 0.0 copy-done.4
  7.3 0.1 copy.15.agg_ref
  7.4 0.0 copy-done.3
  7.4 0.1 reshape.27.keys_ref
  7.5 0.0 copy-done
  7.5 31.5 %shard_map.85 = (f32[32,64,32]{2,1,0:T(8,128)S(1)}, f32[64,32]{1,0:T(8,128)S(1)}, f32[4,4096]{1,0:T(4,128)S(1)}) custom-call(s32[32,3]{1,0:T(8,128)S(1)} %broadcast_subtract_fusion.cols_ref, s32[32,1]{1,0:T(8,128)S(1)} %copy.15.agg_ref, s32[1,96]{1,0:T(1,128)S(1)} %reshape.27.keys_ref, bf16[96,4096]{1,0:T(8,128)(2,1)S(1)} %bitcast.9, ...), custom_call_target="tpu_custom_call" | custom-call | tf_op jit(solution)/shard_map/pallas_call | solution.py:276
  39.0 1.2 %reshape.31 = f32[32,2048]{1,0:T(8,128)} reshape(f32[32,64,32]{2,1,0:T(8,128)S(1)} %get-tuple-element.6) | data formatting | bytes 524288 | tf_op jit(solution)/shard_map/reshape | solution.py:306
  40.2 0.7 %reshape.32 = f32[1,2048]{1,0:T(1,128)} reshape(f32[64,32]{1,0:T(8,128)S(1)} %get-tuple-element.7) | data formatting | bytes 16384 | tf_op jit(solution)/shard_map/reshape | solution.py:307
  40.9 0.6 %copy.17 = f32[1,4,4096]{2,1,0:T(4,128)} copy(f32[1,4,4096]{2,1,0:T(4,128)S(1)} %bitcast.10) | data formatting | bytes 131072
  (3 shorter events, 0.0 us)
Async XLA Ops:
  3.9 2.0 %copy-start.1 = (bf16[32,4096]{1,0:T(8,128)(2,1)S(1)}, bf16[32,4096]{1,0:T(8,128)(2,1)}, u32[]{:S(2)}) copy-start(bf16[32,4096]{1,0:T(8,128)(2,1)} %param.7) | copy-start | bytes 786436
  6.0 0.9 %copy-start.2 = (bf16[32,2048]{1,0:T(8,128)(2,1)S(1)}, bf16[32,2048]{1,0:T(8,128)(2,1)}, u32[]{:S(2)}) copy-start(bf16[32,2048]{1,0:T(8,128)(2,1)} %param.8) | copy-start | bytes 393220
  6.0 1.3 %copy-start.4 = (s32[32,1]{0,1:T(1,128)S(1)}, s32[32,1]{0,1:T(1,128)}, u32[]{:S(2)}) copy-start(s32[32,1]{0,1:T(1,128)} %param.10) | copy-start | bytes 388
  6.0 1.4 %copy-start.3 = (s32[32,3]{0,1:T(4,128)S(1)}, s32[32,3]{0,1:T(4,128)}, u32[]{:S(2)}) copy-start(s32[32,3]{0,1:T(4,128)} %param.11) | copy-start | bytes 1156
  6.0 1.5 %copy-start = (bf16[32,3,4096]{2,0,1:T(8,128)(2,1)S(1)}, bf16[32,3,4096]{2,0,1:T(8,128)(2,1)}, u32[]{:S(2)}) copy-start(bf16[32,3,4096]{2,0,1:T(8,128)(2,1)} %param.6) | copy-start | bytes 2359300

commit v2 on v1

v2 whole, which is shorter than its diff:
```python
import functools

import jax
import jax.numpy as jnp
from jax import lax
from jax.experimental import pallas as pl
from jax.experimental.pallas import tpu as pltpu
from jax.sharding import PartitionSpec as P

TILE = 64
NRHS = 32
KC = 4
SWEEPS = 3
LANES = 128
PITCH = 72
PACK = LANES // NRHS
MESH = pl.DeviceIdType.MESH


def split(value):
    high = value.astype(jnp.bfloat16)
    low = (value - high.astype(jnp.float32)).astype(jnp.bfloat16)
    return high, low


def dot(a, b):
    return jnp.dot(a, b, preferred_element_type=jnp.float32)


def kernel(
    n_gx, n_gy, rows,
    cols_ref, agg_ref, keys_ref, flat_ref, smooth_ref, rhs_ref,
    x_out, cr_out, ct_out,
    ts, fs, bs, xf, tt, ss, xs, xh, halo, xb, rb, acc, rq, part, pair, tin, racc, rin,
    halo_send, halo_recv, pair_send, pair_recv, tile_send, tile_recv, res_send, res_recv,
):
    gx, gy = lax.axis_index("gx"), lax.axis_index("gy")
    me = gx * n_gy + gy
    total = n_gx * n_gy
    half = rows // 2
    groups = rows // PACK
    hgroups = groups // 2
    n_par = n_gy // 2
    parity, mine = lax.rem(gy, 2), lax.div(gy, 2)
    has_left, has_right = me > 0, me < total - 1
    left = (lax.div(me + total - 1, n_gy) % n_gx, lax.rem(me + total - 1, n_gy))
    right = (lax.div(me + 1, n_gy) % n_gx, lax.rem(me + 1, n_gy))
    far_left = jnp.logical_and(gy == 0, gx > 0)
    far_right = jnp.logical_and(gy == n_gy - 1, gx < n_gx - 1)

    barrier = pltpu.get_barrier_semaphore()

    def greet(d, carry):
        pl.semaphore_signal(barrier, inc=1, device_id=(gx, lax.rem(gy + d, n_gy)), device_id_type=MESH)
        return carry

    lax.fori_loop(1, n_gy, greet, 0)

    @pl.when(far_left)
    def _():
        pl.semaphore_signal(barrier, inc=1, device_id=left, device_id_type=MESH)

    @pl.when(far_right)
    def _():
        pl.semaphore_signal(barrier, inc=1, device_id=right, device_id_type=MESH)

    def each(first, last, act):
        def one(d, carry):
            act(d)
            return carry

        lax.fori_loop(first, last, one, 0)

    def square(source, count, spread, target):
        low_lanes = lax.broadcasted_iota(jnp.int32, (count, LANES), 1) < TILE
        for p in range(TILE // 2):
            strip = source[:, LANES * p:LANES * (p + 1)].astype(jnp.float32)
            turned = pltpu.roll(strip, TILE, 1)
            spread[pl.ds(2 * p, count, stride=PITCH), :] = jnp.where(low_lanes, strip, turned)
            spread[pl.ds(2 * p + 1, count, stride=PITCH), :] = jnp.where(low_lanes, turned, strip)
        for t in range(count):
            target[t] = spread[PITCH * t:PITCH * t + TILE, :].astype(jnp.bfloat16)

    def source_block(i):
        return bs[PITCH * i:PITCH * i + TILE, :NRHS]

    def halo_copy(step, side, g):
        return pltpu.make_async_remote_copy(
            src_ref=xh.at[step, side * hgroups + g],
            dst_ref=halo.at[step, 1 - side, g],
            send_sem=halo_send.at[step, side, g],
            recv_sem=halo_recv.at[step, 1 - side, g],
            device_id=left if side == 0 else right,
            device_id_type=MESH,
        )

    def unpack(buffer, packed, first):
        for e in range(PACK):
            xb[buffer, first + e] = packed[:, e * NRHS:(e + 1) * NRHS]

    def update(step, side, g):
        gained = []
        for e in range(PACK):
            i = g * PACK + e
            if step == 0:
                gained.append(dot(ss[i][:, :TILE], source_block(i).astype(jnp.bfloat16)))
            else:
                gained.append(dot(ss[i], rb[i]))
        value = jnp.concatenate(gained, axis=1)
        if step > 0:
            value = xs[step - 1, g] + value
        xs[step, g] = value
        high, low = split(value)
        packed = jnp.concatenate([high, low], axis=0)
        xh[step, g] = packed
        unpack(step % 2, packed, half + g * PACK)
        if step == SWEEPS - 1:
            for e in range(PACK):
                first = PITCH * (g * PACK + e)
                xf[first:first + TILE, :NRHS] = value[:, e * NRHS:(e + 1) * NRHS]

    def update_side(step, side):
        for g in range(hgroups):
            update(step, side, side * hgroups + g)

            @pl.when(has_left if side == 0 else has_right)
            def _():
                halo_copy(step, side, g).start()

    def local_part(step, side):
        for i in range(side * half, (side + 1) * half):
            acc[i] = source_block(i) - dot(tt[i], xb[step % 2, half + i])

    def receive_halo(step, side):
        for g in range(hgroups):
            @pl.when(has_left if side == 0 else has_right)
            def _():
                halo_copy(step, 1 - side, g).wait_recv()

        for g in range(hgroups):
            unpack(step % 2, halo[step, side, g], (0 if side == 0 else half + rows) + g * PACK)

    def residual(step, i):
        one = cols_ref[i, 1]
        two = cols_ref[i, 2]
        return (
            acc[i]
            - dot(tt[rows + i], xb[step % 2, one])
            - dot(tt[2 * rows + i], xb[step % 2, two])
        )

    low_lanes = lax.broadcasted_iota(jnp.int32, (rows, LANES), 1)
    for q in range(TILE // PACK):
        strip = rhs_ref[:, LANES * q:LANES * (q + 1)].astype(jnp.float32)
        for e in range(PACK):
            turned = strip if e == 0 else pltpu.roll(strip, LANES - NRHS * e, 1)
            bs[pl.ds(PACK * q + e, rows, stride=PITCH), :] = turned
    square(smooth_ref, rows, fs, ss)

    waits = n_gy - 1 + far_left.astype(jnp.int32) + far_right.astype(jnp.int32)
    pl.semaphore_wait(barrier, waits)
    update_side(0, 0)
    update_side(0, 1)

    @pl.when(jnp.logical_not(has_left))
    def _():
        halo[:, 0] = jnp.zeros_like(halo[:, 0])

    @pl.when(jnp.logical_not(has_right))
    def _():
        halo[:, 1] = jnp.zeros_like(halo[:, 1])

    square(flat_ref, 3 * rows, ts, tt)

    n_keys = n_gy * KC
    slots = lax.broadcasted_iota(jnp.int32, (n_keys, 3 * rows), 0)
    chosen = jnp.where(slots == keys_ref[...], 1.0, 0.0).astype(jnp.bfloat16)
    width = 1024
    for at in range(0, TILE * TILE, width):
        sums = dot(chosen, flat_ref[:, at:at + width])
        for p in range(2):
            for q in range(n_par):
                row = (p * n_par + q) * KC
                part[p, q, :, at:at + width] = sums[row:row + KC]
    pair_copy = pltpu.make_async_remote_copy(
        src_ref=part.at[1 - parity],
        dst_ref=pair,
        send_sem=pair_send,
        recv_sem=pair_recv,
        device_id=(gx, 2 * mine + 1 - parity),
        device_id_type=MESH,
    )
    pair_copy.start()

    def tile_copy(d):
        target = lax.rem(mine + d, n_par)
        return pltpu.make_async_remote_copy(
            src_ref=part.at[parity, target],
            dst_ref=tin.at[d - 1],
            send_sem=tile_send.at[d - 1],
            recv_sem=tile_recv.at[d - 1],
            device_id=(gx, 2 * target + parity),
            device_id_type=MESH,
        )

    def res_copy(d):
        target = lax.rem(gy + d, n_gy)
        return pltpu.make_async_remote_copy(
            src_ref=racc.at[target],
            dst_ref=rin.at[d - 1],
            send_sem=res_send.at[d - 1],
            recv_sem=res_recv.at[d - 1],
            device_id=(gx, target),
            device_id_type=MESH,
        )

    for side in range(2):
        local_part(0, side)
    for step in range(SWEEPS - 1):
        for side in ((1, 0) if step % 2 == 0 else (0, 1)):
            receive_halo(step, side)
            for i in range(side * half, (side + 1) * half):
                high, low = split(residual(step, i))
                rb[i] = jnp.concatenate([high, low], axis=0)
            update_side(step + 1, side)
        if step == 0:
            pair_copy.wait_recv()

            def join(q):
                part[parity, q] = part[parity, q] + pair[q]

            each(0, n_par, join)
            each(1, n_par, lambda d: tile_copy(d).start())
        for side in range(2):
            local_part(step + 1, side)

    last = SWEEPS - 1
    for q in range(TILE // PACK):
        strips = [xf[pl.ds(PACK * q + e, rows, stride=PITCH), :][:, :NRHS] for e in range(PACK)]
        x_out[:, LANES * q:LANES * (q + 1)] = jnp.concatenate(strips, axis=1)
    ct_out[...] = part[parity, mine]

    def add_tiles(d):
        tile_copy(d).wait_recv()
        ct_out[...] = ct_out[...] + tin[d - 1]

    each(1, n_par, add_tiles)

    quarter = TILE // PACK
    for side in ((1, 0) if last % 2 == 0 else (0, 1)):
        receive_halo(last, side)
        for i in range(side * half, (side + 1) * half):
            value = residual(last, i)
            rq[i] = jnp.concatenate([value[e * quarter:(e + 1) * quarter] for e in range(PACK)], axis=1)

    def gather(a):
        value = jnp.zeros((quarter, LANES), jnp.float32)
        for i in range(rows):
            value = value + jnp.where(agg_ref[i, 0] == a, 1.0, 0.0) * rq[i]
        racc[a] = value

    def gather_send(d):
        gather(lax.rem(gy + d, n_gy))
        res_copy(d).start()

    each(1, n_gy, gather_send)
    gather(gy)

    def add_res(d, value):
        res_copy(d).wait_recv()
        return value + rin[d - 1]

    final = lax.fori_loop(1, n_gy, add_res, racc[gy])
    for e in range(PACK):
        xf[e * quarter:(e + 1) * quarter, :NRHS] = final[:, e * NRHS:(e + 1) * NRHS]
    strips = [xf[pl.ds(e, quarter, stride=PACK), :][:, :NRHS] for e in range(PACK)]
    cr_out[...] = jnp.concatenate(strips, axis=1)

    for step in range(SWEEPS):
        for side in range(2):
            for g in range(hgroups):
                @pl.when(has_left if side == 0 else has_right)
                def _():
                    halo_copy(step, side, g).wait_send()
    pair_copy.wait_send()
    each(1, n_par, lambda d: tile_copy(d).wait_send())
    each(1, n_gy, lambda d: res_copy(d).wait_send())


def body(n_gx, n_gy, tiles, smoother, rhs, cols, agg, coarse_slot):
    rows = tiles.shape[0]
    n_par = n_gy // 2
    groups = rows // PACK
    flat = tiles.transpose(1, 0, 2).reshape(rows * 3, TILE * TILE)
    places = cols - (lax.axis_index(("gx", "gy")) * rows - rows // 2)
    order = (agg % 2) * n_par + agg // 2
    keys = (order * KC + coarse_slot).T.reshape(1, rows * 3)
    vmem = pl.BlockSpec(memory_space=pltpu.VMEM)
    smem = pl.BlockSpec(memory_space=pltpu.SMEM)
    quarter = TILE // PACK
    f32, bf16 = jnp.float32, jnp.bfloat16
    dma = pltpu.SemaphoreType.DMA
    iterate, residual, coarse = pl.pallas_call(
        functools.partial(kernel, n_gx, n_gy, rows),
        out_shape=(
            jax.ShapeDtypeStruct((rows, TILE * NRHS), f32),
            jax.ShapeDtypeStruct((quarter, LANES), f32),
            jax.ShapeDtypeStruct((KC, TILE * TILE), f32),
        ),
        in_specs=[smem, smem, vmem, vmem, vmem, vmem],
        out_specs=(vmem, vmem, vmem),
        scratch_shapes=[
            pltpu.VMEM((3 * rows * PITCH, LANES), f32),
            pltpu.VMEM((rows * PITCH, LANES), f32),
            pltpu.VMEM((rows * PITCH, LANES), f32),
            pltpu.VMEM((rows * PITCH, LANES), f32),
            pltpu.VMEM((3 * rows, TILE, LANES), bf16),
            pltpu.VMEM((rows, TILE, LANES), bf16),
            pltpu.VMEM((SWEEPS, groups, TILE, LANES), f32),
            pltpu.VMEM((SWEEPS, groups, 2 * TILE, LANES), bf16),
            pltpu.VMEM((SWEEPS, 2, groups // 2, 2 * TILE, LANES), bf16),
            pltpu.VMEM((2, 2 * rows, 2 * TILE, NRHS), bf16),
            pltpu.VMEM((rows, 2 * TILE, NRHS), bf16),
            pltpu.VMEM((rows, TILE, NRHS), f32),
            pltpu.VMEM((rows, quarter, LANES), f32),
            pltpu.VMEM((2, n_par, KC, TILE * TILE), f32),
            pltpu.VMEM((n_par, KC, TILE * TILE), f32),
            pltpu.VMEM((n_par - 1, KC, TILE * TILE), f32),
            pltpu.VMEM((n_gy, quarter, LANES), f32),
            pltpu.VMEM((n_gy - 1, quarter, LANES), f32),
            dma((SWEEPS, 2, groups // 2)), dma((SWEEPS, 2, groups // 2)), dma, dma,
            dma((n_par - 1,)), dma((n_par - 1,)), dma((n_gy - 1,)), dma((n_gy - 1,)),
        ],
        compiler_params=pltpu.CompilerParams(
            collective_id=0, has_side_effects=True, vmem_limit_bytes=50 * 1024 * 1024
        ),
    )(places, agg, keys, flat, smoother, rhs)
    return (
        iterate,
        residual.reshape(1, TILE * NRHS),
        coarse.reshape(1, KC, TILE * TILE),
    )


def solution(mesh):
    row_spec = P(("gx", "gy"), None)
    tile_spec = P(("gx", "gy"), None, None)
    return jax.shard_map(
        functools.partial(body, mesh.shape["gx"], mesh.shape["gy"]),
        mesh=mesh,
        in_specs=(tile_spec, row_spec, row_spec, row_spec, row_spec, row_spec),
        out_specs=(row_spec, row_spec, tile_spec),
        check_vma=False,
    )
```

time: 41.7 us -> 40 us (0.959)
  other arithmetic: 2.35 us -> 0.02 us
  Pallas kernels: 31.5 us -> 32.5 us
  local copies, waits for them, and re-layouts: 6.92 us -> 6.44 us
    unnamed x13 -> x17, local copies, waits for them, and re-layouts: 1.54 us -> 6.36 us
    reshape x4 -> x0, local copies, waits for them, and re-layouts: 2.78 us -> none  [the longest x1 1.2 us: body(): iterate.reshape(rows, TILE * NRHS)]
    another operation x1 -> x0, local copies, waits for them, and re-layouts: 2.52 us -> none  [body(): square = flat.reshape(rows * 3, TILE, TILE)]
    concatenate x2 -> x0, other arithmetic: 2.33 us -> none  [the longest x1 2.03 us: body(): double = jnp.concatenate([square, square], axis=2)]
    pallas_call x1, Pallas kernels: 31.5 us -> 32.5 us  [body(): pl.pallas_call(functools.partial(kernel, n_gx, n_gy, rows), out_shape=(ja...]
where the time goes in v2:
time: 40 us; the launch traced here: 39.6 us
  Pallas kernels  32.5 us (81%)
  local copies, waits for them, and re-layouts  6.44 us (16%)
  between operations  0.67 us (2%)
    pallas_call x1, Pallas kernels, body(): pl.pallas_call(functools.partial(kernel, n_gx, n_gy, rows), out_shape=(ja...  32.5 us
    unnamed x17, local copies, waits for them, and re-layouts  6.36 us

profile of v2, /device:TPU:0, one launch (start us, length us, event | category | flops | bytes accessed | tf_op | source)
XLA Modules:
  0.0 39.6 jit_solution(4322224058353946930)
XLA Ops:
  0.6 0.0 copy-start.5
  0.6 0.0 copy-start.4
  0.7 0.6 %copy-done.5 = s32[32,1]{0,1:T(1,128)S(1)} copy-done((s32[32,1]{0,1:T(1,128)S(1)}, s32[32,1]{0,1:T(1,128)}, u32[]{:S(2)}) %copy-start.5) | copy-done | bytes 152
  1.3 0.0 copy-done.4
  1.3 0.0 copy-start.3
  1.3 0.1 reshape.18.keys_ref
  1.4 0.6 %copy-done.3 = s32[32,3]{0,1:T(4,128)S(1)} copy-done((s32[32,3]{0,1:T(4,128)S(1)}, s32[32,3]{0,1:T(4,128)}, u32[]{:S(2)}) %copy-start.3) | copy-done | bytes 408
  2.0 0.1 copy.11
  2.1 0.1 copy.13.agg_ref
  2.2 0.0 copy-start
  2.2 1.1 %copy-done = bf16[32,3,4096]{2,0,1:T(8,128)(2,1)S(1)} copy-done((bf16[32,3,4096]{2,0,1:T(8,128)(2,1)S(1)}, bf16[32,3,4096]{2,0,1:T(8,128)(2,1)}, u32[]{:S(2)}) %copy-start) | copy-done | bytes 786456
  3.3 0.0 copy-start.1
  3.3 0.9 %copy-done.1 = bf16[32,4096]{1,0:T(8,128)(2,1)S(1)} copy-done((bf16[32,4096]{1,0:T(8,128)(2,1)S(1)}, bf16[32,4096]{1,0:T(8,128)(2,1)}, u32[]{:S(2)}) %copy-start.1) | copy-done | bytes 262168
  4.3 0.0 copy-start.2
  4.3 0.9 %copy-done.2 = bf16[32,2048]{1,0:T(8,128)(2,1)S(1)} copy-done((bf16[32,2048]{1,0:T(8,128)(2,1)S(1)}, bf16[32,2048]{1,0:T(8,128)(2,1)}, u32[]{:S(2)}) %copy-start.2) | copy-done | bytes 131096
  5.2 32.5 %shard_map.85 = (f32[32,2048]{1,0:T(8,128)S(1)}, f32[16,128]{1,0:T(8,128)S(1)}, f32[4,4096]{1,0:T(4,128)S(1)}) custom-call(s32[32,3]{1,0:T(8,128)S(1)} %broadcast_subtract_fusion.cols_ref, s32[32,1]{1,0:T(8,128)S(1)} %copy.13.agg_ref, s32[1,96]{1,0:T(1,128)S(1)} %reshape.18.keys_ref, bf16[96,4096]{1,0:T(8,128)(2,1)S(1)} %bitcast.9, ...), custom_call_target="tpu_custom_call" | custom-call | tf_op jit(solution)/shard_map/pallas_call | solution.py:303
  37.7 0.7 %copy.17 = f32[32,2048]{1,0:T(8,128)} copy(f32[32,2048]{1,0:T(8,128)S(1)} %get-tuple-element.12) | data formatting | bytes 524288
  38.4 0.6 %copy.18 = f32[1,2048]{1,0:T(1,128)} copy(f32[1,2048]{1,0:T(1,128)S(1)} %bitcast.11) | data formatting | bytes 16384
  39.0 0.6 %copy.19 = f32[1,4,4096]{2,1,0:T(4,128)} copy(f32[1,4,4096]{2,1,0:T(4,128)S(1)} %bitcast.10) | data formatting | bytes 131072
  (3 shorter events, 0.0 us)
Async XLA Ops:
  0.6 0.7 %copy-start.5 = (s32[32,1]{0,1:T(1,128)S(1)}, s32[32,1]{0,1:T(1,128)}, u32[]{:S(2)}) copy-start(s32[32,1]{0,1:T(1,128)} %param.10) | copy-start | bytes 388
  0.6 0.7 %copy-start.4 = (s32[32,3]{0,1:T(4,128)S(1)}, s32[32,3]{0,1:T(4,128)}, u32[]{:S(2)}) copy-start(s32[32,3]{0,1:T(4,128)} %param.11) | copy-start | bytes 1156
  1.3 0.7 %copy-start.3 = (s32[32,3]{0,1:T(4,128)S(1)}, s32[32,3]{0,1:T(4,128)}, u32[]{:S(2)}) copy-start(s32[32,3]{0,1:T(4,128)} %param.9) | copy-start | bytes 1156
  2.2 1.1 %copy-start = (bf16[32,3,4096]{2,0,1:T(8,128)(2,1)S(1)}, bf16[32,3,4096]{2,0,1:T(8,128)(2,1)}, u32[]{:S(2)}) copy-start(bf16[32,3,4096]{2,0,1:T(8,128)(2,1)} %param.6) | copy-start | bytes 2359300
  3.3 0.9 %copy-start.1 = (bf16[32,4096]{1,0:T(8,128)(2,1)S(1)}, bf16[32,4096]{1,0:T(8,128)(2,1)}, u32[]{:S(2)}) copy-start(bf16[32,4096]{1,0:T(8,128)(2,1)} %smooth_ref.1) | copy-start | bytes 786436
  4.3 0.9 %copy-start.2 = (bf16[32,2048]{1,0:T(8,128)(2,1)S(1)}, bf16[32,2048]{1,0:T(8,128)(2,1)}, u32[]{:S(2)}) copy-start(bf16[32,2048]{1,0:T(8,128)(2,1)} %rhs_ref.1) | copy-start | bytes 393220

commit v3 on v2

--- a/solution.py
+++ b/solution.py
@@ -29,9 +29,9 @@
 
 def kernel(
     n_gx, n_gy, rows,
-    cols_ref, agg_ref, keys_ref, flat_ref, smooth_ref, rhs_ref,
+    cols_ref, agg_ref, keys_ref, flat_hbm, smooth_hbm, rhs_hbm,
     x_out, cr_out, ct_out,
-    ts, fs, bs, xf, tt, ss, xs, xh, halo, xb, rb, acc, rq, part, pair, tin, racc, rin,
+    flat_ref, smooth_ref, rhs_ref, load_sem, ts, fs, bs, xf, tt, ss, xs, xh, halo, xb, rb, acc, rq, part, pair, tin, racc, rin,
     halo_send, halo_recv, pair_send, pair_recv, tile_send, tile_recv, res_send, res_recv,
 ):
     gx, gy = lax.axis_index("gx"), lax.axis_index("gy")
@@ -48,6 +48,12 @@
     far_left = jnp.logical_and(gy == 0, gx > 0)
     far_right = jnp.logical_and(gy == n_gy - 1, gx < n_gx - 1)
 
+    rhs_load = pltpu.make_async_copy(rhs_hbm, rhs_ref, load_sem.at[0])
+    smooth_load = pltpu.make_async_copy(smooth_hbm, smooth_ref, load_sem.at[1])
+    flat_load = pltpu.make_async_copy(flat_hbm, flat_ref, load_sem.at[2])
+    rhs_load.start()
+    smooth_load.start()
+    flat_load.start()
     barrier = pltpu.get_barrier_semaphore()
 
     def greet(d, carry):
@@ -149,12 +155,13 @@
             - dot(tt[2 * rows + i], xb[step % 2, two])
         )
 
-    low_lanes = lax.broadcasted_iota(jnp.int32, (rows, LANES), 1)
+    rhs_load.wait()
     for q in range(TILE // PACK):
         strip = rhs_ref[:, LANES * q:LANES * (q + 1)].astype(jnp.float32)
         for e in range(PACK):
             turned = strip if e == 0 else pltpu.roll(strip, LANES - NRHS * e, 1)
             bs[pl.ds(PACK * q + e, rows, stride=PITCH), :] = turned
+    smooth_load.wait()
     square(smooth_ref, rows, fs, ss)
 
     waits = n_gy - 1 + far_left.astype(jnp.int32) + far_right.astype(jnp.int32)
@@ -170,6 +177,7 @@
     def _():
         halo[:, 1] = jnp.zeros_like(halo[:, 1])
 
+    flat_load.wait()
     square(flat_ref, 3 * rows, ts, tt)
 
     n_keys = n_gy * KC
@@ -296,6 +304,7 @@
     order = (agg % 2) * n_par + agg // 2
     keys = (order * KC + coarse_slot).T.reshape(1, rows * 3)
     vmem = pl.BlockSpec(memory_space=pltpu.VMEM)
+    hbm = pl.BlockSpec(memory_space=pltpu.HBM)
     smem = pl.BlockSpec(memory_space=pltpu.SMEM)
     quarter = TILE // PACK
     f32, bf16 = jnp.float32, jnp.bfloat16
@@ -307,9 +316,13 @@
             jax.ShapeDtypeStruct((quarter, LANES), f32),
             jax.ShapeDtypeStruct((KC, TILE * TILE), f32),
         ),
-        in_specs=[smem, smem, vmem, vmem, vmem, vmem],
+        in_specs=[smem, smem, vmem, hbm, hbm, hbm],
         out_specs=(vmem, vmem, vmem),
         scratch_shapes=[
+            pltpu.VMEM((3 * rows, TILE * TILE), bf16),
+            pltpu.VMEM((rows, TILE * TILE), bf16),
+            pltpu.VMEM((rows, TILE * NRHS), bf16),
+            dma((3,)),
             pltpu.VMEM((3 * rows * PITCH, LANES), f32),
             pltpu.VMEM((rows * PITCH, LANES), f32),
             pltpu.VMEM((rows * PITCH, LANES), f32),
@@ -332,7 +345,7 @@
             dma((n_par - 1,)), dma((n_par - 1,)), dma((n_gy - 1,)), dma((n_gy - 1,)),
         ],
         compiler_params=pltpu.CompilerParams(
-            collective_id=0, has_side_effects=True, vmem_limit_bytes=50 * 1024 * 1024
+            collective_id=0, has_side_effects=True, vmem_limit_bytes=63 * 1024 * 1024
         ),
     )(places, agg, keys, flat, smoother, rhs)
     return (

time: 40 us -> 40 us (level)
  the two profiles are of different devices: /device:TPU:0 before, /device:TPU:3 now
where the time goes in v3:
time: 40 us; the launch traced here: 39.7 us
  Pallas kernels  33.3 us (83%)
  local copies, waits for them, and re-layouts  5.06 us (13%)
  between operations  0.68 us (2%)
  other arithmetic  0.63 us (2%)
    pallas_call x1, Pallas kernels, body(): pl.pallas_call(functools.partial(kernel, n_gx, n_gy, rows), out_shape=(ja...  33.3 us
    unnamed x15, local copies, waits for them, and re-layouts  4.47 us

profile of v3, /device:TPU:3, one launch (start us, length us, event | category | flops | bytes accessed | tf_op | source)
XLA Modules:
  0.0 39.7 jit_solution(6143067531168595807)
XLA Ops:
  0.6 0.0 copy-start.4
  0.6 0.0 copy-start.3
  0.7 0.6 %copy-done.4 = s32[32,1]{0,1:T(1,128)S(1)} copy-done((s32[32,1]{0,1:T(1,128)S(1)}, s32[32,1]{0,1:T(1,128)}, u32[]{:S(2)}) %copy-start.4) | copy-done | bytes 152
  1.3 0.0 copy-done.3
  1.3 0.0 copy-start.2
  1.3 0.6 %reshape.18.keys_ref = s32[1,96]{1,0:T(1,128)} reshape(s32[3,32]{1,0:T(4,128)S(1)} %add_bitcast_fusion) | data formatting | bytes 768 | tf_op jit(solution)/shard_map/reshape | solution.py:305
  1.9 0.1 copy-done.2
  2.0 0.1 copy.11
  2.1 0.6 %broadcast_subtract_fusion.cols_ref = s32[32,3]{1,0:T(8,128)} fusion(s32[32,3]{1,0:T(8,128)S(1)} %copy.11, s32[]{:T(128)S(6)} %sub.15), kind=kLoop, calls=%fused_computation | loop fusion | flops 96 | bytes 772 | tf_op jit(solution)/shard_map/sub | solution.py:303
  2.7 0.7 %copy.13.agg_ref = s32[32,1]{1,0:T(8,128)} copy(s32[32,1]{0,1:T(1,128)S(1)} %copy-done.4) | data formatting | bytes 256 | tf_op args[4]
  3.4 33.3 %shard_map.85 = (f32[32,2048]{1,0:T(8,128)}, f32[16,128]{1,0:T(8,128)}, f32[4,4096]{1,0:T(4,128)}) custom-call(s32[32,3]{1,0:T(8,128)} %broadcast_subtract_fusion.cols_ref, s32[32,1]{1,0:T(8,128)} %copy.13.agg_ref, s32[1,96]{1,0:T(1,128)} %reshape.18.keys_ref, bf16[96,4096]{1,0:T(8,128)(2,1)} %bitcast.9, bf16[32,4096]{1,0:T(8,128)(2,1)} %smooth_hbm.1, ...), custom_call_target="tpu_custom_call" | custom-call | tf_op jit(solution)/shard_map/pallas_call | solution.py:312
  36.8 0.0 copy-start.1
  36.8 0.0 copy-start
  36.8 1.7 %copy.17 = f32[32,2048]{1,0:T(8,128)} copy(f32[32,2048]{1,0:T(8,128)} %get-tuple-element.12) | data formatting | bytes 524288
  38.5 0.0 copy-done.1
  38.5 0.6 %copy.18 = f32[1,2048]{1,0:T(1,128)} copy(f32[1,2048]{1,0:T(1,128)S(1)} %bitcast.11) | data formatting | bytes 16384
  39.1 0.0 copy-done
  39.1 0.6 %copy.19 = f32[1,4,4096]{2,1,0:T(4,128)} copy(f32[1,4,4096]{2,1,0:T(4,128)S(1)} %bitcast.10) | data formatting | bytes 131072
  (2 shorter events, 0.0 us)
Async XLA Ops:
  0.6 0.7 %copy-start.4 = (s32[32,1]{0,1:T(1,128)S(1)}, s32[32,1]{0,1:T(1,128)}, u32[]{:S(2)}) copy-start(s32[32,1]{0,1:T(1,128)} %param.10) | copy-start | bytes 388
  0.6 0.7 %copy-start.3 = (s32[32,3]{0,1:T(4,128)S(1)}, s32[32,3]{0,1:T(4,128)}, u32[]{:S(2)}) copy-start(s32[32,3]{0,1:T(4,128)} %param.11) | copy-start | bytes 1156
  1.3 0.7 %copy-start.2 = (s32[32,3]{0,1:T(4,128)S(1)}, s32[32,3]{0,1:T(4,128)}, u32[]{:S(2)}) copy-start(s32[32,3]{0,1:T(4,128)} %param.9) | copy-start | bytes 1156
  36.8 1.7 %copy-start.1 = (f32[16,128]{1,0:T(8,128)S(1)}, f32[16,128]{1,0:T(8,128)}, u32[]{:S(2)}) copy-start(f32[16,128]{1,0:T(8,128)} %get-tuple-element.7) | copy-start | bytes 24580
  36.8 2.3 %copy-start = (f32[4,4096]{1,0:T(4,128)S(1)}, f32[4,4096]{1,0:T(4,128)}, u32[]{:S(2)}) copy-start(f32[4,4096]{1,0:T(4,128)} %get-tuple-element.8) | copy-start | bytes 196612
